TPU v7x, 32 devices: a whole 2x2x4 slice. The times are simulated.
32 devices in a mesh: redist: 16 (over z, y, x), rep: 2 (over core).
Axes of the slice: x: 2, y: 2, z: 4, core: 2. Of those that a mesh axis runs over, the one named last changes fastest.
Arguments:
- amplitudes: float32 [8, 256, 2, 3840], P(None, 'redist', 'rep'), may hold values from -6 to 6
- integrals: float32 [16, 7680, 2, 1920], P('redist', None, 'rep'), may hold values from -0.0625 to 0.0625
- pair_count: int32 [8], replicated, may hold values from 5760 to 7680, as said below
Outputs:
- cycle_term: float32 [8, 256, 2, 3840], P(None, 'redist', 'rep')
Inputs may be any that keep to these rules, and one draw needn't show every extreme that they name: `pair_count`: each block has at least 5760 live pair slots; some block has all 7680 live.
All inputs are finite; a program needn't handle non-finite values.
Results may differ from a plain program's by a relative error of at most 0.00007.
Values sent between devices are 32-bit elements; how exact they have to be, the bound alone decides.
A program may use at most 128 MiB of HBM per device.

v0:
```python
import jax
import jax.numpy as jnp
from jax import lax
from jax.sharding import PartitionSpec as P

NBLK = 8


def arrange(moved, rows, jb_split, kc_split, col_width, half_slots):
    summed = moved.reshape(NBLK, jb_split, kc_split, rows, col_width).sum(axis=2)
    return summed.transpose(0, 2, 1, 3).reshape(NBLK, rows, 2, half_slots)


def on_device(amplitudes, integrals, pair_count):
    half_slots = amplitudes.shape[3]
    row_count = amplitudes.shape[1]
    col_width = integrals.shape[1]
    kc_width = integrals.shape[3]
    kc_split = half_slots // kc_width
    jb_split = 2 * half_slots // col_width
    device_count = lax.axis_size("redist")
    half_index = lax.axis_index("rep")
    slot_index = half_index * half_slots + lax.iota(jnp.int32, half_slots)
    live_mask = (slot_index[None, :] < pair_count[:, None]).astype(jnp.float32)
    masked = amplitudes[:, :, 0, :] * live_mask[:, None, :]
    pieces = masked.reshape(NBLK, row_count, kc_split, kc_width).transpose(0, 2, 1, 3)
    outgoing = jnp.broadcast_to(
        pieces[:, None], (NBLK, jb_split, kc_split, row_count, kc_width)
    ).reshape(device_count, row_count, kc_width)
    tile_matrix = integrals[0, :, 0, :]
    partial_value = jnp.einsum(
        "srk,jk->srj",
        lax.all_to_all(outgoing, "redist", split_axis=0, concat_axis=0, tiled=True),
        tile_matrix,
        precision=lax.Precision.HIGHEST,
        preferred_element_type=jnp.float32,
    )
    moved = lax.all_to_all(partial_value, "redist", split_axis=0, concat_axis=0, tiled=True)
    arranged = arrange(moved, row_count, jb_split, kc_split, col_width, half_slots)
    result = lax.psum_scatter(arranged, "rep", scatter_dimension=2, tiled=True)
    return result * live_mask[:, None, None, :]


def solution(mesh):
    placed = (P(None, "redist", "rep", None), P("redist", None, "rep", None), P())
    return jax.shard_map(
        on_device,
        mesh=mesh,
        in_specs=placed,
        out_specs=P(None, "redist", "rep", None),
        check_vma=False,
    )
```

profile of v0, /device:TPU:0, one launch (start us, length us, event | category | flops | bytes accessed | tf_op | source)
XLA Modules:
  0.0 336.2 jit_solution(7349675055642595644)
XLA Ops:
  6.5 0.0 reduce-scatter.2.cloned.1.call-start
  6.5 0.7 compare_convert_fusion
  7.3 1.7 bitcast_multiply_fusion
  9.0 0.1 fusion.3
  9.2 0.2 pad_maximum_fusion
  9.3 54.4 %all_to_all.10 = f32[16,16,1920]{2,1,0:T(8,128)S(1)} all-to-all(f32[16,16,1920]{2,1,0:T(8,128)S(1)} %bitcast.15), channel_id=1, replica_groups=mesh['redist'=16,'rep'=2] {'redist'}, dimensions={0} | all-to-all | bytes 3932160 | tf_op jit(solution)/shard_map/all_to_all | solution.py:33
  63.7 71.5 %fusion = f32[16,16,7680]{2,1,0:T(8,128)S(1)} fusion(f32[16,16,1920]{2,1,0:T(8,128)S(1)} %all_to_all.10, f32[1,7680,1,1920]{3,2,1,0:T(1,128)} %param.4), kind=kOutput, calls=%fused_computation | convolution fusion | flops 45298483200 | bytes 68812800 | tf_op jit(solution)/shard_map/srk,jk->srj/dot_general | solution.py:31
  135.2 175.5 %all_to_all.11 = f32[16,16,7680]{2,1,0:T(8,128)S(1)} all-to-all(f32[16,16,7680]{2,1,0:T(8,128)S(1)} %fusion), channel_id=1, replica_groups=mesh['redist'=16,'rep'=2] {'redist'}, dimensions={0} | all-to-all | bytes 15728640 | tf_op jit(solution)/shard_map/all_to_all | solution.py:38
  310.8 0.7 bitcast_reduce_fusion
  311.5 2.3 copy.16
  313.8 0.0 reduce-scatter.2.cloned.1.call-update
  313.8 10.6 %reduce-scatter.2.cloned.1.call-done = f32[8,16,1,3840]{3,1,0,2:T(8,128)} async-done(((f32[8,16,2,3840]{3,1,0,2:T(8,128)}), f32[8,16,1,3840]{3,1,0,2:T(8,128)}) %reduce-scatter.2.cloned.1.call-update) | async-done | bytes 1966096 | tf_op jit(solution)/shard_map/reduce_scatter | solution.py:40
  324.4 1.7 broadcast_multiply_fusion
  326.1 3.3 copy.6
  (1 shorter events, 0.0 us)
Async XLA Ops:
  6.5 317.8 %reduce-scatter.2.cloned.1.call-start = ((), (), s32[]{:S(2)}) async-start(), calls=%async_computation.3 | async-start | bytes 5898240 | tf_op jit(solution)/shard_map/reduce_scatter | solution.py:40
Sparse Core Ops, SparseCore 0:
  313.9 10.4 reduce-scatter.1
where the time goes:
time: 336 us
  blocking collectives  230 us (68%)
  matrix products  71.5 us (21%)
  between operations  13.4 us (4%)
  waiting for transfers between devices  10.6 us (3%)
  local copies, waits for them, and re-layouts  5.73 us (2%)
  other arithmetic  5.03 us (1%)
    all_to_all x1, blocking collectives, on_device(): lax.all_to_all(partial_value, 'redist', split_axis=0, concat_axis=0, tile...  176 us
    dot_general x1, matrix products, on_device(): jnp.einsum('srk,jk->srj', lax.all_to_all(outgoing, 'redist', split_axis=0...  71.5 us
    all_to_all x1, blocking collectives, on_device(): lax.all_to_all(outgoing, 'redist', split_axis=0, concat_axis=0, tiled=True)  54.4 us
    reduce_scatter x1, waiting for transfers between devices, on_device(): result = lax.psum_scatter(arranged, 'rep', scatter_dimension=2, tiled=True)  10.6 us
  transfers between devices with their start and end apart: 1, of which 1 were waited for; matrix products, arithmetic and copies ran while one was open for 0% of the time, Pallas kernels for 0%

commit v1 on v0

--- a/solution.py
+++ b/solution.py
@@ -1,14 +1,266 @@
+import functools
+
 import jax
 import jax.numpy as jnp
 from jax import lax
+from jax.experimental import pallas as pl
+from jax.experimental.pallas import tpu as pltpu
 from jax.sharding import PartitionSpec as P
 
 NBLK = 8
+LANES = 128
+CHUNK = 256
+MESH = pl.DeviceIdType.MESH
 
 
 def arrange(moved, rows, jb_split, kc_split, col_width, half_slots):
     summed = moved.reshape(NBLK, jb_split, kc_split, rows, col_width).sum(axis=2)
     return summed.transpose(0, 2, 1, 3).reshape(NBLK, rows, 2, half_slots)
+
+
+def contract_and_reduce(
+    amp, tiles, out,
+    a_in, a_parts, w_in, w_hi0, w_lo0, w_hi1, w_lo1, rep_out, rep_in, own, x_out, keep, x_in, final,
+    a_send, a_recv, a_local, w_sem, rep_send, rep_recv, x_send, x_recv, o_send, o_recv, o_local,
+):
+    n = 2 * NBLK
+    rows, half = amp.shape[1], amp.shape[2]
+    width = half // 2
+    pieces = width // LANES
+    total = n * rows
+    part = NBLK * rows
+    chunks = half // CHUNK
+    me, core = lax.axis_index("redist"), lax.axis_index("rep")
+    block, mine = me // 2, me % 2
+    place = mine * NBLK + block
+
+    def w_copy(t, slot, which):
+        h = 1 - core if which == 0 else core
+        first = pl.multiple_of((h * half + t * CHUNK) * pieces, 8)
+        return pltpu.make_async_copy(
+            tiles.at[pl.ds(first, CHUNK * pieces), :], w_in.at[slot, which], w_sem.at[slot, which]
+        )
+
+    def a_piece(tile):
+        return amp.at[tile // 2, :, pl.ds(pl.multiple_of((tile % 2) * width, LANES), width)]
+
+    def a_copy(tile):
+        return pltpu.make_async_remote_copy(
+            src_ref=a_piece(tile), dst_ref=a_in.at[place],
+            send_sem=a_send.at[tile], recv_sem=a_recv.at[place],
+            device_id=(tile, core), device_id_type=MESH,
+        )
+
+    def a_arrival(source):
+        return pltpu.make_async_remote_copy(
+            src_ref=a_piece(source), dst_ref=a_in.at[source % 2 * NBLK + source // 2],
+            send_sem=a_send.at[source], recv_sem=a_recv.at[source % 2 * NBLK + source // 2],
+            device_id=(source, core), device_id_type=MESH,
+        )
+
+    def far(i):
+        return (1 - me // NBLK) * NBLK + (me + i) % NBLK
+
+    def near(i):
+        return me // NBLK * NBLK + (me + i) % NBLK
+
+    for which in range(2):
+        w_copy(0, 0, which).start()
+    local = pltpu.make_async_copy(a_piece(me), a_in.at[place], a_local)
+    local.start()
+
+    barrier = pltpu.get_barrier_semaphore()
+    pl.semaphore_signal(barrier, inc=1, device_id=(me, 1 - core), device_id_type=MESH)
+
+    @pl.loop(1, n)
+    def _(i):
+        pl.semaphore_signal(barrier, inc=1, device_id=((me + i) % n, core), device_id_type=MESH)
+
+    pl.semaphore_wait(barrier, n)
+
+    @pl.loop(0, NBLK)
+    def _(i):
+        a_copy(far(i)).start()
+
+    @pl.loop(1, NBLK)
+    def _(i):
+        a_copy(near(i)).start()
+
+    def split_rows(at):
+        first = pl.multiple_of(at * rows, rows)
+        value = a_in[at]
+        high = value.astype(jnp.bfloat16)
+        a_parts[pl.ds(first, rows), :] = high
+        a_parts[pl.ds(total + first, rows), :] = (value - high.astype(jnp.float32)).astype(jnp.bfloat16)
+
+    local.wait()
+    split_rows(place)
+
+    @pl.loop(1, NBLK)
+    def _(i):
+        source = near(i)
+        a_arrival(source).wait_recv()
+        split_rows(source % 2 * NBLK + source // 2)
+
+    @pl.loop(0, NBLK)
+    def _(i):
+        source = far(i)
+        a_arrival(source).wait_recv()
+        split_rows(source % 2 * NBLK + source // 2)
+
+    def rep_copy(t):
+        return pltpu.make_async_remote_copy(
+            src_ref=rep_out.at[t], dst_ref=rep_in.at[t],
+            send_sem=rep_send.at[t], recv_sem=rep_recv.at[t],
+            device_id=(me, 1 - core), device_id_type=MESH,
+        )
+
+    def x_copy(t):
+        return pltpu.make_async_remote_copy(
+            src_ref=x_out.at[t], dst_ref=x_in.at[t],
+            send_sem=x_send.at[t], recv_sem=x_recv.at[t],
+            device_id=(block * 2 + 1 - mine, core), device_id_type=MESH,
+        )
+
+    def o_dst(t):
+        return out.at[block, :, pl.ds(pl.multiple_of(t * CHUNK, CHUNK), CHUNK)]
+
+    def o_src(t, owner):
+        return final.at[t, pl.ds(pl.multiple_of(owner * rows, rows), rows), :]
+
+    def o_copy(t, owner):
+        return pltpu.make_async_remote_copy(
+            src_ref=o_src(t, owner), dst_ref=o_dst(t),
+            send_sem=o_send.at[owner], recv_sem=o_recv.at[block],
+            device_id=(owner * 2 + mine, core), device_id_type=MESH,
+        )
+
+    contract = functools.partial(
+        lax.dot_general, dimension_numbers=(((1,), (1,)), ((), ())), preferred_element_type=jnp.float32
+    )
+
+    def product(slot, which, w_hi, w_lo):
+        source = w_in.at[slot, which]
+        for c in range(pieces):
+            at = slice(c * LANES, (c + 1) * LANES)
+            value = source[pl.ds(c, CHUNK, stride=pieces), :]
+            high = value.astype(jnp.bfloat16)
+            w_hi[:, at] = high
+            w_lo[:, at] = (value - high.astype(jnp.float32)).astype(jnp.bfloat16)
+        first = contract(a_parts[...], w_hi[...])
+        second = contract(a_parts[:total, :], w_lo[...])
+        return first[:total] + (first[total:] + second)
+
+    def multiply(t):
+        slot = t % 2
+
+        @pl.when(t + 1 < chunks)
+        def _():
+            w_copy(t + 1, 1 - slot, 0).start()
+            w_copy(t + 1, 1 - slot, 1).start()
+
+        w_copy(t, slot, 0).wait()
+        rep_out[t] = product(slot, 0, w_hi0, w_lo0)
+        rep_copy(t).start()
+        w_copy(t, slot, 1).wait()
+        own[slot] = product(slot, 1, w_hi1, w_lo1)
+
+    def sum_cores(t):
+        slot = t % 2
+        rep_copy(t).wait_recv()
+        there = pl.ds(pl.multiple_of((1 - mine) * part, part), part)
+        here = pl.ds(pl.multiple_of(mine * part, part), part)
+        x_out[t] = own[slot, there, :] + rep_in[t, there, :]
+        x_copy(t).start()
+        keep[t % 4] = own[slot, here, :] + rep_in[t, here, :]
+
+    def sum_pieces(t):
+        x_copy(t).wait_recv()
+        final[t] = keep[t % 4] + x_in[t]
+
+        @pl.loop(0, NBLK // 2)
+        def _(i):
+            o_copy(t, (1 - block // 4) * 4 + (block + i) % 4).start()
+
+        @pl.loop(1, NBLK // 2)
+        def _(i):
+            o_copy(t, block // 4 * 4 + (block + i) % 4).start()
+
+        pltpu.make_async_copy(o_src(t, block), o_dst(t), o_local).start()
+
+    @pl.loop(0, chunks + 3)
+    def _(t):
+        @pl.when((t >= 1) & (t < chunks + 1))
+        def _():
+            sum_cores(t - 1)
+
+        @pl.when(t < chunks)
+        def _():
+            multiply(t)
+
+        @pl.when(t >= 3)
+        def _():
+            sum_pieces(t - 3)
+
+    @pl.loop(0, chunks)
+    def _(t):
+        rep_copy(t).wait_send()
+        x_copy(t).wait_send()
+
+    @pl.loop(1, n)
+    def _(i):
+        a_copy((me + i) % n).wait_send()
+
+    pltpu.make_async_copy(out.at[block], out.at[block], o_local).wait()
+
+    @pl.loop(1, NBLK)
+    def _(i):
+        owner = (block + i) % NBLK
+        pltpu.make_async_remote_copy(
+            src_ref=out.at[owner], dst_ref=out.at[owner],
+            send_sem=o_send.at[owner], recv_sem=o_recv.at[owner],
+            device_id=(owner * 2 + mine, core), device_id_type=MESH,
+        ).wait()
+
+
+def fused(masked, tiles):
+    rows, half = masked.shape[1], masked.shape[2]
+    width = half // 2
+    total, part, chunks = 2 * NBLK * rows, NBLK * rows, half // CHUNK
+    f32, bf16, dma = jnp.float32, jnp.bfloat16, pltpu.SemaphoreType.DMA
+    return pl.pallas_call(
+        contract_and_reduce,
+        out_shape=jax.ShapeDtypeStruct(masked.shape, f32),
+        in_specs=[pl.BlockSpec(memory_space=pl.ANY)] * 2,
+        out_specs=pl.BlockSpec(memory_space=pl.ANY),
+        scratch_shapes=[
+            pltpu.VMEM((2 * NBLK, rows, width), f32),
+            pltpu.VMEM((2 * total, width), bf16),
+            pltpu.VMEM((2, 2, CHUNK * width // LANES, LANES), f32),
+            pltpu.VMEM((CHUNK, width), bf16),
+            pltpu.VMEM((CHUNK, width), bf16),
+            pltpu.VMEM((CHUNK, width), bf16),
+            pltpu.VMEM((CHUNK, width), bf16),
+            pltpu.VMEM((chunks, total, CHUNK), f32),
+            pltpu.VMEM((chunks, total, CHUNK), f32),
+            pltpu.VMEM((2, total, CHUNK), f32),
+            pltpu.VMEM((chunks, part, CHUNK), f32),
+            pltpu.VMEM((4, part, CHUNK), f32),
+            pltpu.VMEM((chunks, part, CHUNK), f32),
+            pltpu.VMEM((chunks, part, CHUNK), f32),
+            dma((2 * NBLK,)), dma((2 * NBLK,)), dma,
+            dma((2, 2)),
+            dma((chunks,)), dma((chunks,)),
+            dma((chunks,)), dma((chunks,)),
+            dma((NBLK,)), dma((NBLK,)), dma,
+        ],
+        compiler_params=pltpu.CompilerParams(
+            collective_id=0, has_side_effects=True, vmem_limit_bytes=50 * 1024 * 1024
+        ),
+        cost_estimate=pl.CostEstimate(
+            flops=6 * total * width * 2 * half, bytes_accessed=tiles.size * 4, transcendentals=0
+        ),
+    )(masked, tiles)
 
 
 def on_device(amplitudes, integrals, pair_count):
@@ -23,6 +275,12 @@
     slot_index = half_index * half_slots + lax.iota(jnp.int32, half_slots)
     live_mask = (slot_index[None, :] < pair_count[:, None]).astype(jnp.float32)
     masked = amplitudes[:, :, 0, :] * live_mask[:, None, :]
+    if (
+        jb_split == 1 and kc_split == 2 and device_count == 2 * NBLK
+        and row_count % 16 == 0 and half_slots % CHUNK == 0 and kc_width % LANES == 0
+    ):
+        result = fused(masked, integrals.reshape(-1, LANES))
+        return (result * live_mask[:, None, :])[:, :, None, :]
     pieces = masked.reshape(NBLK, row_count, kc_split, kc_width).transpose(0, 2, 1, 3)
     outgoing = jnp.broadcast_to(
         pieces[:, None], (NBLK, jb_split, kc_split, row_count, kc_width)

time: 336 us -> 129 us (0.38)
  blocking collectives: 230 us -> 0 us
  Pallas kernels: 0 us -> 123 us
  matrix products: 71.5 us -> 0 us
  between operations: 13.4 us -> 0.02 us
  waiting for transfers between devices: 10.6 us -> 0 us
    all_to_all x2 -> x0, blocking collectives: 230 us -> none  [the longest x1 176 us: on_device(): lax.all_to_all(partial_value, 'redist', split_axis=0, concat_axis=0, tile...]
    pallas_call x0 -> x1, Pallas kernels: none -> 123 us  [fused(): pl.pallas_call(contract_and_reduce, out_shape=jax.ShapeDtypeStruct(masked...]
    dot_general x1 -> x0, matrix products: 71.5 us -> none  [on_device(): jnp.einsum('srk,jk->srj', lax.all_to_all(outgoing, 'redist', split_axis=0...]
    reduce_scatter x1 -> x0, waiting for transfers between devices: 10.6 us -> none  [on_device(): result = lax.psum_scatter(arranged, 'rep', scatter_dimension=2, tiled=True)]
  transfers between devices with their start and end apart: 1 -> 0, of which waited for: 1 -> 0; matrix products, arithmetic and copies ran while one was open for 0% -> 0% of each run, Pallas kernels for 0% -> 0%
where the time goes in v1:
time: 129 us
  Pallas kernels  123 us (95%)
  local copies, waits for them, and re-layouts  3.29 us (3%)
  other arithmetic  2.64 us (2%)
    pallas_call x1, Pallas kernels, fused(): pl.pallas_call(contract_and_reduce, out_shape=jax.ShapeDtypeStruct(masked...  123 us
    broadcast_in_dim x1, local copies, waits for them, and re-layouts, on_device(): return (result * live_mask[:, None, :])[:, :, None, :]  3.29 us

profile of v1, /device:TPU:0, one launch (start us, length us, event | category | flops | bytes accessed | tf_op | source)
XLA Modules:
  0.0 129.1 jit_solution(1110169305510008900)
XLA Ops:
  0.0 0.7 compare_convert_fusion
  0.7 1.7 %bitcast_multiply_fusion.amp = f32[8,16,3840]{2,1,0:T(8,128)S(1)} fusion(f32[8,16,1,3840]{3,2,1,0:T(1,128)} %param.3, f32[8,3840]{1,0:T(8,128)S(1)} %compare_convert_fusion), kind=kLoop, calls=%fused_computation | loop fusion | flops 491520 | bytes 4055040 | tf_op jit(solution)/shard_map/mul | solution.py:277
  2.5 123.1 %shard_map.37 = f32[8,16,3840]{2,1,0:T(8,128)S(1)} custom-call(f32[8,16,3840]{2,1,0:T(8,128)S(1)} %bitcast_multiply_fusion.amp, f32[115200,128]{1,0:T(8,128)} %bitcast.5), custom_call_target="tpu_custom_call" | custom-call | flops 22649241600 | bytes 58982400 | tf_op jit(solution)/shard_map/pallas_call | solution.py:231
  125.6 0.2 multiply_bitcast_fusion
  125.8 3.3 %copy.4 = f32[8,16,1,3840]{3,2,1,0:T(1,128)} copy(f32[8,16,1,3840]{3,1,0,2:T(8,128)S(1)} %multiply_bitcast_fusion) | data formatting | bytes 3932160 | tf_op jit(solution)/shard_map/broadcast_in_dim | solution.py:283
  (1 shorter events, 0.0 us)

commit v2 on v0

--- a/solution.py
+++ b/solution.py
@@ -1,14 +1,302 @@
 import jax
 import jax.numpy as jnp
 from jax import lax
+from jax.experimental import pallas as pl
+from jax.experimental.pallas import tpu as pltpu
 from jax.sharding import PartitionSpec as P
 
 NBLK = 8
+LANES = 128
+CHUNK = 256
+MESH = pl.DeviceIdType.MESH
 
 
 def arrange(moved, rows, jb_split, kc_split, col_width, half_slots):
     summed = moved.reshape(NBLK, jb_split, kc_split, rows, col_width).sum(axis=2)
     return summed.transpose(0, 2, 1, 3).reshape(NBLK, rows, 2, half_slots)
+
+
+def contract_and_reduce(
+    amp, tiles, out,
+    a_in, a_parts, w_in, w_kept, w_now0, w_now1, rep_out, rep_in, own, x_out, keep, x_in, final,
+    a_send, a_recv, a_local, w_sem, rep_send, rep_recv, x_send, x_recv, o_send, o_recv, o_local,
+):
+    n = 2 * NBLK
+    zone = NBLK // 2
+    rows, half = amp.shape[1], amp.shape[2]
+    width = half // 2
+    pieces = width // LANES
+    part = NBLK * rows
+    chunks = half // CHUNK
+    kept = w_kept.shape[0]
+    me, core = lax.axis_index("redist"), lax.axis_index("rep")
+    block, mine = me // 2, me % 2
+
+    def position(owner):
+        return (owner // NBLK + me // NBLK) % 2 * NBLK + owner % 2 * zone + owner // 2 % zone
+
+    def w_copy(u, which):
+        h = 1 - core if which == 0 else core
+        t = jnp.where(u < chunks, u, u - (chunks - kept))
+        first = pl.multiple_of((h * half + t * CHUNK) * pieces, 8)
+        return pltpu.make_async_copy(
+            tiles.at[pl.ds(first, CHUNK * pieces), :], w_in.at[u % 2, which], w_sem.at[u % 2, which]
+        )
+
+    def a_piece(tile):
+        return amp.at[tile // 2, :, pl.ds(pl.multiple_of((tile % 2) * width, LANES), width)]
+
+    def a_slot(at):
+        return a_in.at[pl.ds(pl.multiple_of(at * rows, rows), rows), :]
+
+    def a_copy(tile):
+        at = (tile // NBLK + me // NBLK) % 2 * NBLK + mine * zone + block % zone
+        return pltpu.make_async_remote_copy(
+            src_ref=a_piece(tile), dst_ref=a_slot(at),
+            send_sem=a_send.at[tile], recv_sem=a_recv.at[at],
+            device_id=(tile, core), device_id_type=MESH,
+        )
+
+    def a_arrival(source):
+        return pltpu.make_async_remote_copy(
+            src_ref=a_piece(source), dst_ref=a_slot(position(source)),
+            send_sem=a_send.at[source], recv_sem=a_recv.at[position(source)],
+            device_id=(source, core), device_id_type=MESH,
+        )
+
+    def far(i):
+        return (1 - me // NBLK) * NBLK + (me + i) % NBLK
+
+    def near(i):
+        return me // NBLK * NBLK + (me + i) % NBLK
+
+    w_copy(0, 0).start()
+    w_copy(0, 1).start()
+    local = pltpu.make_async_copy(a_piece(me), a_slot(position(me)), a_local)
+    local.start()
+
+    barrier = pltpu.get_barrier_semaphore()
+    pl.semaphore_signal(barrier, inc=1, device_id=(me, 1 - core), device_id_type=MESH)
+
+    @pl.loop(1, n)
+    def _(i):
+        pl.semaphore_signal(barrier, inc=1, device_id=((me + i) % n, core), device_id_type=MESH)
+
+    pl.semaphore_wait(barrier, n)
+
+    @pl.loop(1, NBLK)
+    def _(i):
+        a_copy(near(i)).start()
+        a_copy(far(i)).start()
+
+    a_copy(far(0)).start()
+
+    def split(u, which, w_parts):
+        w_copy(u, which).wait()
+        source = w_in.at[u % 2, which]
+        for c in range(pieces):
+            at = slice(c * LANES, (c + 1) * LANES)
+            value = source[pl.ds(c, CHUNK, stride=pieces), :]
+            high = value.astype(jnp.bfloat16)
+            w_parts[:CHUNK, at] = high
+            w_parts[CHUNK:, at] = (value - high.astype(jnp.float32)).astype(jnp.bfloat16)
+
+    def fetch(u):
+        w_copy(u, 0).start()
+        w_copy(u, 1).start()
+
+    @pl.loop(0, kept)
+    def _(t):
+        fetch(t + 1)
+        split(t, 0, w_kept.at[t, 0])
+        split(t, 1, w_kept.at[t, 1])
+
+    def split_rows(group):
+        for c in range(pieces):
+            at = slice(c * LANES, (c + 1) * LANES)
+            value = a_in[group * part:(group + 1) * part, at].T
+            high = value.astype(jnp.bfloat16)
+            a_parts[group, at, :part] = high
+            a_parts[group, at, part:] = (value - high.astype(jnp.float32)).astype(jnp.bfloat16)
+
+    def rep_copy(q):
+        return pltpu.make_async_remote_copy(
+            src_ref=rep_out.at[q], dst_ref=rep_in.at[q],
+            send_sem=rep_send.at[q], recv_sem=rep_recv.at[q],
+            device_id=(me, 1 - core), device_id_type=MESH,
+        )
+
+    def x_copy(q):
+        return pltpu.make_async_remote_copy(
+            src_ref=x_out.at[q], dst_ref=x_in.at[q],
+            send_sem=x_send.at[q], recv_sem=x_recv.at[q],
+            device_id=(block * 2 + 1 - mine, core), device_id_type=MESH,
+        )
+
+    def o_dst(q):
+        return out.at[block, :, pl.ds(pl.multiple_of(q % chunks * CHUNK, CHUNK), CHUNK)]
+
+    def o_src(q, owner):
+        return final.at[q, pl.ds(pl.multiple_of(owner % zone * rows, rows), rows), :]
+
+    def o_copy(q, owner):
+        return pltpu.make_async_remote_copy(
+            src_ref=o_src(q, owner), dst_ref=o_dst(q),
+            send_sem=o_send.at[owner], recv_sem=o_recv.at[block],
+            device_id=(owner * 2 + mine, core), device_id_type=MESH,
+        )
+
+    def product(w_parts, group):
+        value = jnp.dot(w_parts[...], a_parts[group], preferred_element_type=jnp.float32)
+        high = value[:CHUNK, :part]
+        low = value[CHUNK:, :part] + value[:CHUNK, part:]
+        return high + (low + value[CHUNK:, part:])
+
+    def sum_cores(q):
+        value = (own[q % 2] + rep_in[q]).T
+        first, second = value[:part // 2], value[part // 2:]
+        x_out[q] = jnp.where(mine == 0, second, first)
+        x_copy(q).start()
+        keep[q % 4] = jnp.where(mine == 0, first, second)
+
+    def sum_pieces(q):
+        x_copy(q).wait_recv()
+        final[q] = keep[q % 4] + x_in[q]
+        group = q // chunks
+        side = (block // zone + group) % 2 * zone
+
+        @pl.when(group == 0)
+        def _():
+            pltpu.make_async_copy(o_src(q, block), o_dst(q), o_local).start()
+
+        @pl.when(group == 1)
+        def _():
+            o_copy(q, side + block % zone).start()
+
+        @pl.loop(1, zone)
+        def _(i):
+            o_copy(q, side + (block + i) % zone).start()
+
+    def settle(q):
+        @pl.when(q >= 1)
+        def _():
+            rep_copy(q - 1).wait_recv()
+            sum_cores(q - 1)
+
+    def deliver(q):
+        @pl.when(q >= 3)
+        def _():
+            sum_pieces(q - 3)
+
+    def work(group):
+        @pl.loop(group * chunks, group * chunks + kept)
+        def _(q):
+            settle(q)
+            t = q - group * chunks
+            rep_out[q] = product(w_kept.at[t, 0], group)
+            rep_copy(q).start()
+            own[q % 2] = product(w_kept.at[t, 1], group)
+            deliver(q)
+
+        @pl.loop(group * chunks + kept, (group + 1) * chunks)
+        def _(q):
+            settle(q)
+            u = q - group * kept
+
+            @pl.when(u + 1 < 2 * chunks - kept)
+            def _():
+                fetch(u + 1)
+
+            split(u, 0, w_now0)
+            rep_out[q] = product(w_now0, group)
+            rep_copy(q).start()
+            split(u, 1, w_now1)
+            own[q % 2] = product(w_now1, group)
+            deliver(q)
+
+    local.wait()
+
+    @pl.loop(1, NBLK)
+    def _(i):
+        a_arrival(near(i)).wait_recv()
+
+    split_rows(0)
+    work(0)
+
+    @pl.loop(0, NBLK)
+    def _(i):
+        a_arrival(far(i)).wait_recv()
+
+    split_rows(1)
+    work(1)
+
+    steps = 2 * chunks
+    rep_copy(steps - 1).wait_recv()
+    sum_cores(steps - 1)
+
+    @pl.loop(steps - 3, steps)
+    def _(q):
+        sum_pieces(q)
+
+    @pl.loop(0, steps)
+    def _(q):
+        rep_copy(q).wait_send()
+        x_copy(q).wait_send()
+
+    @pl.loop(1, n)
+    def _(i):
+        a_copy((me + i) % n).wait_send()
+
+    pltpu.make_async_copy(out.at[block], out.at[block], o_local).wait()
+
+    @pl.loop(1, NBLK)
+    def _(i):
+        owner = (block + i) % NBLK
+        pltpu.make_async_remote_copy(
+            src_ref=out.at[owner], dst_ref=out.at[owner],
+            send_sem=o_send.at[owner], recv_sem=o_recv.at[owner],
+            device_id=(owner * 2 + mine, core), device_id_type=MESH,
+        ).wait()
+
+
+def fused(masked, tiles):
+    rows, half = masked.shape[1], masked.shape[2]
+    width = half // 2
+    total, part, chunks = 2 * NBLK * rows, NBLK * rows, half // CHUNK
+    kept, steps = chunks // 2, 2 * chunks
+    f32, bf16, dma = jnp.float32, jnp.bfloat16, pltpu.SemaphoreType.DMA
+    return pl.pallas_call(
+        contract_and_reduce,
+        out_shape=jax.ShapeDtypeStruct(masked.shape, f32),
+        in_specs=[pl.BlockSpec(memory_space=pl.ANY)] * 2,
+        out_specs=pl.BlockSpec(memory_space=pl.ANY),
+        scratch_shapes=[
+            pltpu.VMEM((total, width), f32),
+            pltpu.VMEM((2, width, 2 * part), bf16),
+            pltpu.VMEM((2, 2, CHUNK * width // LANES, LANES), f32),
+            pltpu.VMEM((kept, 2, 2 * CHUNK, width), bf16),
+            pltpu.VMEM((2 * CHUNK, width), bf16),
+            pltpu.VMEM((2 * CHUNK, width), bf16),
+            pltpu.VMEM((steps, CHUNK, part), f32),
+            pltpu.VMEM((steps, CHUNK, part), f32),
+            pltpu.VMEM((2, CHUNK, part), f32),
+            pltpu.VMEM((steps, part // 2, CHUNK), f32),
+            pltpu.VMEM((4, part // 2, CHUNK), f32),
+            pltpu.VMEM((steps, part // 2, CHUNK), f32),
+            pltpu.VMEM((steps, part // 2, CHUNK), f32),
+            dma((2 * NBLK,)), dma((2 * NBLK,)), dma,
+            dma((2, 2)),
+            dma((steps,)), dma((steps,)),
+            dma((steps,)), dma((steps,)),
+            dma((NBLK,)), dma((NBLK,)), dma,
+        ],
+        compiler_params=pltpu.CompilerParams(
+            collective_id=0, has_side_effects=True, vmem_limit_bytes=60 * 1024 * 1024
+        ),
+        cost_estimate=pl.CostEstimate(
+            flops=8 * total * width * 2 * half, bytes_accessed=tiles.size * 6, transcendentals=0
+        ),
+    )(masked, tiles)
 
 
 def on_device(amplitudes, integrals, pair_count):
@@ -23,6 +311,12 @@
     slot_index = half_index * half_slots + lax.iota(jnp.int32, half_slots)
     live_mask = (slot_index[None, :] < pair_count[:, None]).astype(jnp.float32)
     masked = amplitudes[:, :, 0, :] * live_mask[:, None, :]
+    if (
+        jb_split == 1 and kc_split == 2 and device_count == 2 * NBLK
+        and row_count * NBLK == LANES and half_slots % CHUNK == 0 and kc_width % LANES == 0
+    ):
+        result = fused(masked, integrals.reshape(-1, LANES))
+        return (result * live_mask[:, None, :])[:, :, None, :]
     pieces = masked.reshape(NBLK, row_count, kc_split, kc_width).transpose(0, 2, 1, 3)
     outgoing = jnp.broadcast_to(
         pieces[:, None], (NBLK, jb_split, kc_split, row_count, kc_width)

time: 336 us -> 142 us (0.42)
  blocking collectives: 230 us -> 0 us
  Pallas kernels: 0 us -> 131 us
  matrix products: 71.5 us -> 0 us
  between operations: 13.4 us -> 0.02 us
  waiting for transfers between devices: 10.6 us -> 0 us
    all_to_all x2 -> x0, blocking collectives: 230 us -> none  [the longest x1 176 us: on_device(): lax.all_to_all(partial_value, 'redist', split_axis=0, concat_axis=0, tile...]
    pallas_call x0 -> x1, Pallas kernels: none -> 131 us  [fused(): pl.pallas_call(contract_and_reduce, out_shape=jax.ShapeDtypeStruct(masked...]
    dot_general x1 -> x0, matrix products: 71.5 us -> none  [on_device(): jnp.einsum('srk,jk->srj', lax.all_to_all(outgoing, 'redist', split_axis=0...]
    reduce_scatter x1 -> x0, waiting for transfers between devices: 10.6 us -> none  [on_device(): result = lax.psum_scatter(arranged, 'rep', scatter_dimension=2, tiled=True)]
  transfers between devices with their start and end apart: 1 -> 0, of which waited for: 1 -> 0; matrix products, arithmetic and copies ran while one was open for 0% -> 0% of each run, Pallas kernels for 0% -> 0%
where the time goes in v2:
time: 142 us; the launch traced here: 139 us
  Pallas kernels  131 us (92%)
  other arithmetic  5.45 us (4%)
  local copies, waits for them, and re-layouts  3.29 us (2%)
    pallas_call x1, Pallas kernels, fused(): pl.pallas_call(contract_and_reduce, out_shape=jax.ShapeDtypeStruct(masked...  131 us
    broadcast_in_dim x1, local copies, waits for them, and re-layouts, on_device(): return (result * live_mask[:, None, :])[:, :, None, :]  3.29 us
    mul x1, other arithmetic, on_device(): masked = amplitudes[:, :, 0, :] * live_mask[:, None, :]  3.01 us

profile of v2, /device:TPU:0, one launch (start us, length us, event | category | flops | bytes accessed | tf_op | source)
XLA Modules:
  0.0 139.4 jit_solution(8497252132178881000)
XLA Ops:
  0.0 0.7 compare_convert_fusion
  0.7 3.0 %bitcast_multiply_fusion.amp = f32[8,16,3840]{2,1,0:T(8,128)} fusion(f32[8,16,1,3840]{3,2,1,0:T(1,128)} %param.3, f32[8,3840]{1,0:T(8,128)S(1)} %compare_convert_fusion), kind=kLoop, calls=%fused_computation | loop fusion | flops 491520 | bytes 4055040 | tf_op jit(solution)/shard_map/mul | solution.py:313
  3.8 130.6 %shard_map.37 = f32[8,16,3840]{2,1,0:T(8,128)} custom-call(f32[8,16,3840]{2,1,0:T(8,128)} %bitcast_multiply_fusion.amp, f32[115200,128]{1,0:T(8,128)} %bitcast.5), custom_call_target="tpu_custom_call" | custom-call | flops 30198988800 | bytes 88473600 | tf_op jit(solution)/shard_map/pallas_call | solution.py:268
  134.4 1.7 %multiply_bitcast_fusion = f32[8,16,1,3840]{3,1,0,2:T(8,128)S(1)} fusion(f32[8,16,3840]{2,1,0:T(8,128)} %shard_map.37, f32[8,3840]{1,0:T(8,128)S(1)} %compare_convert_fusion), kind=kLoop, calls=%fused_computation.1 | loop fusion | flops 491520 | bytes 4055040 | tf_op jit(solution)/shard_map/broadcast_in_dim | solution.py:319
  136.1 3.3 %copy.4 = f32[8,16,1,3840]{3,2,1,0:T(1,128)} copy(f32[8,16,1,3840]{3,1,0,2:T(8,128)S(1)} %multiply_bitcast_fusion) | data formatting | bytes 3932160 | tf_op jit(solution)/shard_map/broadcast_in_dim | solution.py:319
  (1 shorter events, 0.0 us)

commit v3 on v1

--- a/solution.py
+++ b/solution.py
@@ -19,9 +19,9 @@
 
 
 def contract_and_reduce(
-    amp, tiles, out,
-    a_in, a_parts, w_in, w_hi0, w_lo0, w_hi1, w_lo1, rep_out, rep_in, own, x_out, keep, x_in, final,
-    a_send, a_recv, a_local, w_sem, rep_send, rep_recv, x_send, x_recv, o_send, o_recv, o_local,
+    amp, tiles, out, w_spill,
+    a_in, a_parts, w_in, w_kept, w_stage, rep_out, rep_in, own, x_out, keep, x_in, final,
+    a_send, a_recv, a_local, w_sem, w_store, w_load, rep_send, rep_recv, x_send, x_recv, o_send, o_recv, o_local,
 ):
     n = 2 * NBLK
     rows, half = amp.shape[1], amp.shape[2]
@@ -30,6 +30,7 @@
     total = n * rows
     part = NBLK * rows
     chunks = half // CHUNK
+    kept = w_kept.shape[0]
     me, core = lax.axis_index("redist"), lax.axis_index("rep")
     block, mine = me // 2, me % 2
     place = mine * NBLK + block
@@ -85,6 +86,59 @@
     @pl.loop(1, NBLK)
     def _(i):
         a_copy(near(i)).start()
+
+    def split(t, which, w_parts):
+        w_copy(t, t % 2, which).wait()
+        source = w_in.at[t % 2, which]
+        for c in range(pieces):
+            at = slice(c * LANES, (c + 1) * LANES)
+            value = source[pl.ds(c, CHUNK, stride=pieces), :]
+            high = value.astype(jnp.bfloat16)
+            w_parts[:CHUNK, at] = high
+            w_parts[CHUNK:, at] = (value - high.astype(jnp.float32)).astype(jnp.bfloat16)
+
+    def fetch(t):
+        @pl.when(t < chunks)
+        def _():
+            w_copy(t, t % 2, 0).start()
+            w_copy(t, t % 2, 1).start()
+
+    def store(t, which):
+        return pltpu.make_async_copy(
+            w_stage.at[t % 2, which], w_spill.at[t - kept, which], w_store.at[t % 2, which]
+        )
+
+    def load(t, which):
+        return pltpu.make_async_copy(
+            w_spill.at[t - kept, which], w_stage.at[t % 2, which], w_load.at[t % 2, which]
+        )
+
+    @pl.loop(0, kept)
+    def _(t):
+        fetch(t + 1)
+        split(t, 0, w_kept.at[t, 0])
+        split(t, 1, w_kept.at[t, 1])
+
+    @pl.loop(kept, chunks)
+    def _(t):
+        fetch(t + 1)
+
+        @pl.when(t >= kept + 2)
+        def _():
+            store(t - 2, 0).wait()
+            store(t - 2, 1).wait()
+
+        split(t, 0, w_stage.at[t % 2, 0])
+        store(t, 0).start()
+        split(t, 1, w_stage.at[t % 2, 1])
+        store(t, 1).start()
+
+    for t in (chunks - 2, chunks - 1):
+        store(t, 0).wait()
+        store(t, 1).wait()
+
+    load(kept, 0).start()
+    load(kept, 1).start()
 
     def split_rows(at):
         first = pl.multiple_of(at * rows, rows)
@@ -139,35 +193,18 @@
         lax.dot_general, dimension_numbers=(((1,), (1,)), ((), ())), preferred_element_type=jnp.float32
     )
 
-    def product(slot, which, w_hi, w_lo):
-        source = w_in.at[slot, which]
-        for c in range(pieces):
-            at = slice(c * LANES, (c + 1) * LANES)
-            value = source[pl.ds(c, CHUNK, stride=pieces), :]
-            high = value.astype(jnp.bfloat16)
-            w_hi[:, at] = high
-            w_lo[:, at] = (value - high.astype(jnp.float32)).astype(jnp.bfloat16)
-        first = contract(a_parts[...], w_hi[...])
-        second = contract(a_parts[:total, :], w_lo[...])
+    def product(w_parts):
+        first = contract(a_parts[...], w_parts[:CHUNK, :])
+        second = contract(a_parts[:total, :], w_parts[CHUNK:, :])
         return first[:total] + (first[total:] + second)
 
-    def multiply(t):
-        slot = t % 2
-
-        @pl.when(t + 1 < chunks)
-        def _():
-            w_copy(t + 1, 1 - slot, 0).start()
-            w_copy(t + 1, 1 - slot, 1).start()
-
-        w_copy(t, slot, 0).wait()
-        rep_out[t] = product(slot, 0, w_hi0, w_lo0)
+    def multiply(t, w_parts):
+        rep_out[t] = product(w_parts.at[0])
         rep_copy(t).start()
-        w_copy(t, slot, 1).wait()
-        own[slot] = product(slot, 1, w_hi1, w_lo1)
+        own[t % 2] = product(w_parts.at[1])
 
     def sum_cores(t):
         slot = t % 2
-        rep_copy(t).wait_recv()
         there = pl.ds(pl.multiple_of((1 - mine) * part, part), part)
         here = pl.ds(pl.multiple_of(mine * part, part), part)
         x_out[t] = own[slot, there, :] + rep_in[t, there, :]
@@ -188,19 +225,43 @@
 
         pltpu.make_async_copy(o_src(t, block), o_dst(t), o_local).start()
 
-    @pl.loop(0, chunks + 3)
-    def _(t):
-        @pl.when((t >= 1) & (t < chunks + 1))
-        def _():
+    def settle(t):
+        @pl.when(t >= 1)
+        def _():
+            rep_copy(t - 1).wait_recv()
             sum_cores(t - 1)
 
-        @pl.when(t < chunks)
-        def _():
-            multiply(t)
-
+    def deliver(t):
         @pl.when(t >= 3)
         def _():
             sum_pieces(t - 3)
+
+    @pl.loop(0, kept)
+    def _(t):
+        settle(t)
+        multiply(t, w_kept.at[t])
+        deliver(t)
+
+    @pl.loop(kept, chunks)
+    def _(t):
+        settle(t)
+
+        @pl.when(t + 1 < chunks)
+        def _():
+            load(t + 1, 0).start()
+            load(t + 1, 1).start()
+
+        load(t, 0).wait()
+        load(t, 1).wait()
+        multiply(t, w_stage.at[t % 2])
+        deliver(t)
+
+    rep_copy(chunks - 1).wait_recv()
+    sum_cores(chunks - 1)
+
+    @pl.loop(chunks - 3, chunks)
+    def _(t):
+        sum_pieces(t)
 
     @pl.loop(0, chunks)
     def _(t):
@@ -227,20 +288,22 @@
     rows, half = masked.shape[1], masked.shape[2]
     width = half // 2
     total, part, chunks = 2 * NBLK * rows, NBLK * rows, half // CHUNK
+    kept = chunks * 2 // 5
     f32, bf16, dma = jnp.float32, jnp.bfloat16, pltpu.SemaphoreType.DMA
-    return pl.pallas_call(
+    result, _ = pl.pallas_call(
         contract_and_reduce,
-        out_shape=jax.ShapeDtypeStruct(masked.shape, f32),
+        out_shape=(
+            jax.ShapeDtypeStruct(masked.shape, f32),
+            jax.ShapeDtypeStruct((chunks - kept, 2, 2 * CHUNK, width), bf16),
+        ),
         in_specs=[pl.BlockSpec(memory_space=pl.ANY)] * 2,
-        out_specs=pl.BlockSpec(memory_space=pl.ANY),
+        out_specs=[pl.BlockSpec(memory_space=pl.ANY)] * 2,
         scratch_shapes=[
             pltpu.VMEM((2 * NBLK, rows, width), f32),
             pltpu.VMEM((2 * total, width), bf16),
             pltpu.VMEM((2, 2, CHUNK * width // LANES, LANES), f32),
-            pltpu.VMEM((CHUNK, width), bf16),
-            pltpu.VMEM((CHUNK, width), bf16),
-            pltpu.VMEM((CHUNK, width), bf16),
-            pltpu.VMEM((CHUNK, width), bf16),
+            pltpu.VMEM((kept, 2, 2 * CHUNK, width), bf16),
+            pltpu.VMEM((2, 2, 2 * CHUNK, width), bf16),
             pltpu.VMEM((chunks, total, CHUNK), f32),
             pltpu.VMEM((chunks, total, CHUNK), f32),
             pltpu.VMEM((2, total, CHUNK), f32),
@@ -249,18 +312,19 @@
             pltpu.VMEM((chunks, part, CHUNK), f32),
             pltpu.VMEM((chunks, part, CHUNK), f32),
             dma((2 * NBLK,)), dma((2 * NBLK,)), dma,
-            dma((2, 2)),
+            dma((2, 2)), dma((2, 2)), dma((2, 2)),
             dma((chunks,)), dma((chunks,)),
             dma((chunks,)), dma((chunks,)),
             dma((NBLK,)), dma((NBLK,)), dma,
         ],
         compiler_params=pltpu.CompilerParams(
-            collective_id=0, has_side_effects=True, vmem_limit_bytes=50 * 1024 * 1024
+            collective_id=0, has_side_effects=True, vmem_limit_bytes=60 * 1024 * 1024
         ),
         cost_estimate=pl.CostEstimate(
             flops=6 * total * width * 2 * half, bytes_accessed=tiles.size * 4, transcendentals=0
         ),
     )(masked, tiles)
+    return result
 
 
 def on_device(amplitudes, integrals, pair_count):
@@ -277,7 +341,7 @@
     masked = amplitudes[:, :, 0, :] * live_mask[:, None, :]
     if (
         jb_split == 1 and kc_split == 2 and device_count == 2 * NBLK
-        and row_count % 16 == 0 and half_slots % CHUNK == 0 and kc_width % LANES == 0
+        and row_count % 16 == 0 and half_slots >= 5 * CHUNK and half_slots % CHUNK == 0 and kc_width % LANES == 0
     ):
         result = fused(masked, integrals.reshape(-1, LANES))
         return (result * live_mask[:, None, :])[:, :, None, :]

time: 129 us -> 131 us (1.016)
  other arithmetic: 2.64 us -> 5.45 us
    broadcast_in_dim x1, other arithmetic: 0.16 us -> 1.71 us  [on_device(): return (result * live_mask[:, None, :])[:, :, None, :]]
where the time goes in v3:
time: 131 us
  Pallas kernels  122 us (93%)
  other arithmetic  5.45 us (4%)
  local copies, waits for them, and re-layouts  3.29 us (3%)
    pallas_call x1, Pallas kernels, fused(): pl.pallas_call(contract_and_reduce, out_shape=(jax.ShapeDtypeStruct(maske...  122 us
    broadcast_in_dim x1, local copies, waits for them, and re-layouts, on_device(): return (result * live_mask[:, None, :])[:, :, None, :]  3.29 us
    mul x1, other arithmetic, on_device(): masked = amplitudes[:, :, 0, :] * live_mask[:, None, :]  3.01 us

profile of v3, /device:TPU:0, one launch (start us, length us, event | category | flops | bytes accessed | tf_op | source)
XLA Modules:
  0.0 130.8 jit_solution(4284185054723256840)
XLA Ops:
  0.0 0.7 compare_convert_fusion
  0.7 3.0 %bitcast_multiply_fusion.amp = f32[8,16,3840]{2,1,0:T(8,128)} fusion(f32[8,16,1,3840]{3,2,1,0:T(1,128)} %param.3, f32[8,3840]{1,0:T(8,128)S(1)} %compare_convert_fusion), kind=kLoop, calls=%fused_computation | loop fusion | flops 491520 | bytes 4055040 | tf_op jit(solution)/shard_map/mul | solution.py:341
  3.8 122.0 %shard_map.37 = (f32[8,16,3840]{2,1,0:T(8,128)}, bf16[9,2,512,1920]{3,2,1,0:T(8,128)(2,1)}) custom-call(f32[8,16,3840]{2,1,0:T(8,128)} %bitcast_multiply_fusion.amp, f32[115200,128]{1,0:T(8,128)} %bitcast.5), custom_call_target="tpu_custom_call" | custom-call | flops 22649241600 | bytes 58982400 | tf_op jit(solution)/shard_map/pallas_call | solution.py:293
  125.8 1.7 %multiply_bitcast_fusion = f32[8,16,1,3840]{3,1,0,2:T(8,128)S(1)} fusion(f32[8,16,3840]{2,1,0:T(8,128)} %get-tuple-element.6, f32[8,3840]{1,0:T(8,128)S(1)} %compare_convert_fusion), kind=kLoop, calls=%fused_computation.1 | loop fusion | flops 491520 | bytes 4055040 | tf_op jit(solution)/shard_map/broadcast_in_dim | solution.py:347
  127.5 3.3 %copy.4 = f32[8,16,1,3840]{3,2,1,0:T(1,128)} copy(f32[8,16,1,3840]{3,1,0,2:T(8,128)S(1)} %multiply_bitcast_fusion) | data formatting | bytes 3932160 | tf_op jit(solution)/shard_map/broadcast_in_dim | solution.py:347
  (1 shorter events, 0.0 us)

commit v4 on v3

--- a/solution.py
+++ b/solution.py
@@ -31,6 +31,7 @@
     part = NBLK * rows
     chunks = half // CHUNK
     kept = w_kept.shape[0]
+    depth = a_parts.shape[1]
     me, core = lax.axis_index("redist"), lax.axis_index("rep")
     block, mine = me // 2, me % 2
     place = mine * NBLK + block
@@ -96,6 +97,8 @@
             high = value.astype(jnp.bfloat16)
             w_parts[:CHUNK, at] = high
             w_parts[CHUNK:, at] = (value - high.astype(jnp.float32)).astype(jnp.bfloat16)
+        if depth > width:
+            w_parts[:, width:] = jnp.zeros((2 * CHUNK, depth - width), jnp.bfloat16)
 
     def fetch(t):
         @pl.when(t < chunks)
@@ -105,12 +108,12 @@
 
     def store(t, which):
         return pltpu.make_async_copy(
-            w_stage.at[t % 2, which], w_spill.at[t - kept, which], w_store.at[t % 2, which]
+            w_stage.at[t % 2, which, :, pl.ds(0, width)], w_spill.at[t - kept, which], w_store.at[t % 2, which]
         )
 
     def load(t, which):
         return pltpu.make_async_copy(
-            w_spill.at[t - kept, which], w_stage.at[t % 2, which], w_load.at[t % 2, which]
+            w_spill.at[t - kept, which], w_stage.at[t % 2, which, :, pl.ds(0, width)], w_load.at[t % 2, which]
         )
 
     @pl.loop(0, kept)
@@ -144,9 +147,11 @@
         first = pl.multiple_of(at * rows, rows)
         value = a_in[at]
         high = value.astype(jnp.bfloat16)
-        a_parts[pl.ds(first, rows), :] = high
-        a_parts[pl.ds(total + first, rows), :] = (value - high.astype(jnp.float32)).astype(jnp.bfloat16)
-
+        a_parts[pl.ds(first, rows), :width] = high
+        a_parts[pl.ds(total + first, rows), :width] = (value - high.astype(jnp.float32)).astype(jnp.bfloat16)
+
+    if depth > width:
+        a_parts[:, width:] = jnp.zeros((2 * total, depth - width), jnp.bfloat16)
     local.wait()
     split_rows(place)
 
@@ -201,6 +206,7 @@
     def multiply(t, w_parts):
         rep_out[t] = product(w_parts.at[0])
         rep_copy(t).start()
+        deliver(t)
         own[t % 2] = product(w_parts.at[1])
 
     def sum_cores(t):
@@ -232,15 +238,14 @@
             sum_cores(t - 1)
 
     def deliver(t):
-        @pl.when(t >= 3)
-        def _():
-            sum_pieces(t - 3)
+        @pl.when(t >= 2)
+        def _():
+            sum_pieces(t - 2)
 
     @pl.loop(0, kept)
     def _(t):
         settle(t)
         multiply(t, w_kept.at[t])
-        deliver(t)
 
     @pl.loop(kept, chunks)
     def _(t):
@@ -254,12 +259,11 @@
         load(t, 0).wait()
         load(t, 1).wait()
         multiply(t, w_stage.at[t % 2])
-        deliver(t)
 
     rep_copy(chunks - 1).wait_recv()
     sum_cores(chunks - 1)
 
-    @pl.loop(chunks - 3, chunks)
+    @pl.loop(chunks - 2, chunks)
     def _(t):
         sum_pieces(t)
 
@@ -288,7 +292,8 @@
     rows, half = masked.shape[1], masked.shape[2]
     width = half // 2
     total, part, chunks = 2 * NBLK * rows, NBLK * rows, half // CHUNK
-    kept = chunks * 2 // 5
+    kept = chunks // 3
+    depth = (width + CHUNK - 1) // CHUNK * CHUNK
     f32, bf16, dma = jnp.float32, jnp.bfloat16, pltpu.SemaphoreType.DMA
     result, _ = pl.pallas_call(
         contract_and_reduce,
@@ -300,10 +305,10 @@
         out_specs=[pl.BlockSpec(memory_space=pl.ANY)] * 2,
         scratch_shapes=[
             pltpu.VMEM((2 * NBLK, rows, width), f32),
-            pltpu.VMEM((2 * total, width), bf16),
+            pltpu.VMEM((2 * total, depth), bf16),
             pltpu.VMEM((2, 2, CHUNK * width // LANES, LANES), f32),
-            pltpu.VMEM((kept, 2, 2 * CHUNK, width), bf16),
-            pltpu.VMEM((2, 2, 2 * CHUNK, width), bf16),
+            pltpu.VMEM((kept, 2, 2 * CHUNK, depth), bf16),
+            pltpu.VMEM((2, 2, 2 * CHUNK, depth), bf16),
             pltpu.VMEM((chunks, total, CHUNK), f32),
             pltpu.VMEM((chunks, total, CHUNK), f32),
             pltpu.VMEM((2, total, CHUNK), f32),

time: 131 us -> 129 us (0.985)
  Pallas kernels: 122 us -> 120 us
    pallas_call x1, Pallas kernels: 122 us -> 120 us  [fused(): pl.pallas_call(contract_and_reduce, out_shape=(jax.ShapeDtypeStruct(maske...]
where the time goes in v4:
time: 129 us
  Pallas kernels  120 us (93%)
  other arithmetic  5.45 us (4%)
  local copies, waits for them, and re-layouts  3.29 us (3%)
    pallas_call x1, Pallas kernels, fused(): pl.pallas_call(contract_and_reduce, out_shape=(jax.ShapeDtypeStruct(maske...  120 us
    broadcast_in_dim x1, local copies, waits for them, and re-layouts, on_device(): return (result * live_mask[:, None, :])[:, :, None, :]  3.29 us
    mul x1, other arithmetic, on_device(): masked = amplitudes[:, :, 0, :] * live_mask[:, None, :]  3.01 us

profile of v4, /device:TPU:0, one launch (start us, length us, event | category | flops | bytes accessed | tf_op | source)
XLA Modules:
  0.0 128.6 jit_solution(331207168618249412)
XLA Ops:
  0.0 0.7 compare_convert_fusion
  0.7 3.0 %bitcast_multiply_fusion.amp = f32[8,16,3840]{2,1,0:T(8,128)} fusion(f32[8,16,1,3840]{3,2,1,0:T(1,128)} %param.3, f32[8,3840]{1,0:T(8,128)S(1)} %compare_convert_fusion), kind=kLoop, calls=%fused_computation | loop fusion | flops 491520 | bytes 4055040 | tf_op jit(solution)/shard_map/mul | solution.py:346
  3.8 119.9 %shard_map.37 = (f32[8,16,3840]{2,1,0:T(8,128)}, bf16[10,2,512,1920]{3,2,1,0:T(8,128)(2,1)}) custom-call(f32[8,16,3840]{2,1,0:T(8,128)} %bitcast_multiply_fusion.amp, f32[115200,128]{1,0:T(8,128)} %bitcast.5), custom_call_target="tpu_custom_call" | custom-call | flops 22649241600 | bytes 58982400 | tf_op jit(solution)/shard_map/pallas_call | solution.py:298
  123.6 1.7 %multiply_bitcast_fusion = f32[8,16,1,3840]{3,1,0,2:T(8,128)S(1)} fusion(f32[8,16,3840]{2,1,0:T(8,128)} %get-tuple-element.6, f32[8,3840]{1,0:T(8,128)S(1)} %compare_convert_fusion), kind=kLoop, calls=%fused_computation.1 | loop fusion | flops 491520 | bytes 4055040 | tf_op jit(solution)/shard_map/broadcast_in_dim | solution.py:352
  125.3 3.3 %copy.4 = f32[8,16,1,3840]{3,2,1,0:T(1,128)} copy(f32[8,16,1,3840]{3,1,0,2:T(8,128)S(1)} %multiply_bitcast_fusion) | data formatting | bytes 3932160 | tf_op jit(solution)/shard_map/broadcast_in_dim | solution.py:352
  (1 shorter events, 0.0 us)
